TPU v7x, 32 devices: a whole 2x2x4 slice. The times are simulated.
32 devices in a mesh: dp: 16 (over z, y, x), mp: 2 (over core).
Axes of the slice: x: 2, y: 2, z: 4, core: 2. Of those that a mesh axis runs over, the one named last changes fastest.
Arguments:
- tokens: bfloat16 [16384, 768], P(('dp', 'mp')), may hold values from -6 to 6
- lengths: int32 [32, 8], P('dp'), may hold values from 1 to 256, 512 in all within a row
- cotangent: bfloat16 [16384, 768], P(('dp', 'mp')), may hold values from -6 to 6
- triple_weight: bfloat16 [768, 3, 768], P(None, None, 'mp'), may hold values from -0.21875 to 0.21875
- query_value_bias: bfloat16 [2, 768], P(None, 'mp'), may hold values from -3 to 3
- output_weight: bfloat16 [768, 768], P('mp'), may hold values from -0.875 to 0.875
- branch_bias: bfloat16 [2, 768], replicated, may hold values from -2 to 2
- expand_weight: bfloat16 [768, 3072], P(None, 'mp'), may hold values from -0.21875 to 0.21875
- expand_bias: bfloat16 [3072], P('mp'), may hold values from -2 to 2
- shrink_weight: bfloat16 [3072, 768], P('mp'), may hold values from -0.109375 to 0.109375
- adapter_down: float32 [2, 768, 64], replicated, may hold values from -0.21875 to 0.21875
- down_bias: float32 [2, 64], replicated, may hold values from -2 to 2
- adapter_up: float32 [2, 64, 768], replicated, may hold values from -0.75 to 0.75
- up_bias: float32 [2, 768], replicated, may hold values from -2 to 2
- norm_params: float32 [4, 768], replicated, may hold values from -1.2 to 1.4, as said below
- adapter_down_first: float32 [2, 768, 64], replicated, may hold values from -0.00390625 to 0.00390625
- adapter_down_second: float32 [2, 768, 64], replicated, may hold values from 2.4833122e-09 to 3.9732996e-08
- down_bias_first: float32 [2, 64], replicated, may hold values from -0.00390625 to 0.00390625
- down_bias_second: float32 [2, 64], replicated, may hold values from 2.4833122e-09 to 3.9732996e-08
- adapter_up_first: float32 [2, 64, 768], replicated, may hold values from -0.00390625 to 0.00390625
- adapter_up_second: float32 [2, 64, 768], replicated, may hold values from 2.4833122e-09 to 3.9732996e-08
- up_bias_first: float32 [2, 768], replicated, may hold values from -0.00390625 to 0.00390625
- up_bias_second: float32 [2, 768], replicated, may hold values from 7.449936e-10 to 5.959949e-09
- norm_params_first: float32 [4, 768], replicated, may hold values from -0.00390625 to 0.00390625
- norm_params_second: float32 [4, 768], replicated, may hold values from 2.4833122e-09 to 3.9732996e-08
- step: int32 [1], replicated, may hold values from 2 to 5
Outputs:
- output: float32 [16384, 768], P(('dp', 'mp'))
- input_grad: float32 [16384, 768], P(('dp', 'mp'))
- grad_norm: float32 [1], replicated
- adapter_down_new: float32 [2, 768, 64], replicated
- adapter_down_first_new: float32 [2, 768, 64], replicated
- adapter_down_second_new: float32 [2, 768, 64], replicated
- down_bias_new: float32 [2, 64], replicated
- down_bias_first_new: float32 [2, 64], replicated
- down_bias_second_new: float32 [2, 64], replicated
- adapter_up_new: float32 [2, 64, 768], replicated
- adapter_up_first_new: float32 [2, 64, 768], replicated
- adapter_up_second_new: float32 [2, 64, 768], replicated
- up_bias_new: float32 [2, 768], replicated
- up_bias_first_new: float32 [2, 768], replicated
- up_bias_second_new: float32 [2, 768], replicated
- norm_params_new: float32 [4, 768], replicated
- norm_params_first_new: float32 [4, 768], replicated
- norm_params_second_new: float32 [4, 768], replicated
Inputs may be any that keep to these rules, and one draw needn't show every extreme that they name: Each packed row of 512 tokens holds 8 pairs back to back whose lengths sum to 512; some pair in the batch has exactly 256 tokens. `norm_params`: rows 0 and 2 are gains, rows 1 and 3 shifts.
All inputs are finite; a program needn't handle non-finite values.
Results may differ from a plain program's by a relative error of at most 0.018.
Values may be sent and summed in bfloat16 or wider, within the bound.
A program may use at most 128 MiB of HBM per device.

v0:
```python
import functools
import types

import jax
import jax.numpy as jnp
from jax import lax
from jax.experimental import pallas as pl
from jax.experimental.pallas import tpu as pltpu
from jax.sharding import PartitionSpec as P

HEAD_DIM = 64
SLOTS = 8
EPSILON = 1e-12
CLIP_LIMIT = 1.0
LOG2E = 1.4426950408889634
HALF_ROOT = 0.7071067811865476
DENSITY = 0.3989422804014327
NEGATIVE = -1e30
RATES = ((0.03, 0.01), (0.1, 0.0), (0.1, 0.01), (0.1, 0.0), (0.2, 0.0))
PART = 80
MESH = pl.DeviceIdType.MESH
BF = jnp.bfloat16
F32 = jnp.float32


def nn(a, b):
    return lax.dot_general(a, b, (((1,), (0,)), ((), ())), preferred_element_type=F32)


def nt(a, b):
    return lax.dot_general(a, b, (((1,), (1,)), ((), ())), preferred_element_type=F32)


def tn(a, b):
    return lax.dot_general(a, b, (((0,), (0,)), ((), ())), preferred_element_type=F32)


def at(start, size, step=None):
    if isinstance(start, int):
        return pl.ds(start, size)
    return pl.ds(pl.multiple_of(start, step or size), size)


def gelu_parts(value):
    mass = 0.5 + 0.5 * lax.erf(value * HALF_ROOT)
    slope = mass + value * (jnp.exp2(value * value * (-0.5 * LOG2E)) * DENSITY)
    return value * mass, slope


def fold_rows(value):
    rows, width = value.shape
    return jnp.sum(value.reshape(rows // 8, 8, width), axis=0)


SCRATCH = (
    ("xs", lambda z: ((z.tok, z.width), BF)),
    ("cots", lambda z: ((z.tok, z.width), BF)),
    ("w3", lambda z: ((z.width, 6 * z.half), BF)),
    ("wo", lambda z: ((2 * z.half, z.width), BF)),
    ("we", lambda z: ((z.width, z.ff), BF)),
    ("ws", lambda z: ((z.ff, z.width), BF)),
    ("down_l", lambda z: ((2, 64, z.width), BF)),
    ("up_l", lambda z: ((2, 64, z.width), BF)),
    ("bias_own", lambda z: ((8, z.ff_half), F32)),
    ("bias_far", lambda z: ((8, z.ff_half), F32)),
    ("keys", lambda z: ((z.tok, z.width), BF)),
    ("values", lambda z: ((z.tok, z.width), BF)),
    ("q_t", lambda z: ((z.width, z.tok), BF)),
    ("k_t", lambda z: ((z.width, z.tok), BF)),
    ("v_t", lambda z: ((z.width, z.tok), BF)),
    ("hot", lambda z: ((z.tok, 128), BF)),
    ("qa", lambda z: ((4 * 256, z.tok), BF)),
    ("ex", lambda z: ((z.heads, z.tok, z.tok), BF)),
    ("fac", lambda z: ((z.heads, 8, z.tok), F32)),
    ("o_t", lambda z: ((z.width, z.tok), BF)),
    ("att", lambda z: ((z.tok, z.width), BF)),
    ("br_l", lambda z: ((2, z.tok, z.width), BF)),
    ("act", lambda z: ((2, z.tok, 128), BF)),
    ("gd", lambda z: ((2, z.tok, 64), F32)),
    ("inl", lambda z: ((z.tok, 64), BF)),
    ("normed", lambda z: ((z.tok, z.width), F32)),
    ("scale_s", lambda z: ((z.tok, 1), F32)),
    ("first_f", lambda z: ((z.tok, z.width), F32)),
    ("first_l", lambda z: ((z.tok, z.width), BF)),
    ("hid", lambda z: ((z.tok, z.ff), BF)),
    ("slope", lambda z: ((z.tok, z.ff), BF)),
    ("tmp", lambda z: ((z.tok, z.width), F32)),
    ("grads", lambda z: ((2, 2, PART, z.width), F32)),
    ("acc", lambda z: ((48, z.width), F32)),
    ("c_recv", lambda z: ((2, PART, z.width), F32)),
    ("rs_buf", lambda z: ((2, z.n_dp, z.piece, 128), BF)),
    ("rs_recv", lambda z: ((2, z.n_dp - 1, z.piece, 128), BF)),
    ("ag_buf", lambda z: ((2, z.n_dp, z.piece, 128), BF)),
    ("ag_far", lambda z: ((2, z.n_dp, z.piece, 128), BF)),
)
SEMAPHORES = (
    ("load_sem", 25),
    ("meet", 0),
    ("far_send", 7),
    ("far_recv", 7),
    ("core_send", 4),
    ("core_recv", 4),
    ("ring_send", 4),
    ("ring_recv", 4),
)
INPUTS = (
    ("lengths", "s"),
    ("qv_bias", "v"),
    ("branch_bias", "v"),
    ("expand_bias", "v"),
    ("down_bias", "v"),
    ("up_bias", "v"),
    ("norms", "v"),
    ("tokens", "h"),
    ("cot", "h"),
    ("triple", "h"),
    ("out_w", "h"),
    ("expand", "h"),
    ("shrink", "h"),
    *((f"param{index}", "h") for index in range(15)),
)
CHUNK = 256
SUB = 32


def weave(*works):
    queues = [[list(work), 0] for work in works]
    most = max(len(queue[0]) for queue in queues)
    for tick in range(most):
        for queue in queues:
            units, done = queue
            goal = -(-len(units) * (tick + 1) // most)
            for unit in units[done:goal]:
                unit()
            queue[1] = max(done, goal)


def normalize(v):
    center = v - jnp.mean(v, axis=-1, keepdims=True)
    scale = lax.rsqrt(jnp.mean(center * center, axis=-1, keepdims=True) + EPSILON)
    return center * scale, scale


def set_masks(z, r, ends):
    def marks(shape, axis):
        place = lax.broadcasted_iota(jnp.int32, shape, axis)
        found = jnp.zeros(shape, jnp.int32)
        for end in ends:
            found = found + (place >= end).astype(jnp.int32)
        return found

    tok = z.tok
    r.hot[...] = jnp.where(
        marks((tok, 128), 0) == lax.broadcasted_iota(jnp.int32, (tok, 128), 1), 1.0, 0.0
    ).astype(BF)
    shut = jnp.where(
        marks((128, tok), 1) == lax.broadcasted_iota(jnp.int32, (128, tok), 0), 0.0, NEGATIVE
    ).astype(BF)
    for slot in range(4):
        r.qa[at(slot * 256, 128), :] = jnp.zeros((128, tok), BF)
        r.qa[at(slot * 256 + 128, 128), :] = shut


def project(z, r, side):
    bias = (r.bias_own, r.bias_far)[side]
    base = side * 3 * z.half
    rows = at(side * z.half, z.half)
    for c in range(3):
        mixed = nn(r.xs[...], r.w3[:, at(base + c * z.half, z.half)])
        if c == 0:
            mixed = mixed + bias[0:1, 0 : z.half]
        if c == 2:
            mixed = mixed + bias[1:2, 0 : z.half]
        low = mixed.astype(BF)
        if c == 0:
            r.q_t[rows, :] = (low.astype(F32) * (HEAD_DIM ** -0.5)).astype(BF).T
        if c == 1:
            r.keys[:, rows] = low
            r.k_t[rows, :] = low.T
        if c == 2:
            r.values[:, rows] = low
            r.v_t[rows, :] = low.T


def attend(z, r, side):
    span = z.tok // 2
    first = side * z.half // HEAD_DIM
    count = z.half // HEAD_DIM
    ones = jnp.ones((16, z.tok), BF)
    kept = {}

    def scores(head):
        slot = head % 4
        r.qa[at(slot * 256 + (head % 2) * 64, 64), :] = r.q_t[at(head * 64, 64), :]
        keys = jnp.concatenate([r.keys[:, at(head // 2 * 128, 128)], r.hot[...]], axis=1)
        peaks = []
        for kh in range(2):
            tops = []
            for c in range(2):
                s = nn(keys[kh * span : (kh + 1) * span], r.qa[at(slot * 256, 256), at(c * span, span)])
                top = jnp.max(s, axis=0, keepdims=True) * LOG2E
                r.ex[head, at(kh * span, span), at(c * span, span)] = jnp.exp2(
                    s * LOG2E - top
                ).astype(BF)
                tops.append(top)
            peaks.append(jnp.concatenate(tops, axis=1))
        kept[head] = peaks

    def gather(head):
        rows = at(head * 64, 64)
        values = jnp.concatenate([r.v_t[rows, :], ones], axis=0)
        parts = [
            nn(values[:, kh * span : (kh + 1) * span], r.ex[head, at(kh * span, span), :])
            for kh in range(2)
        ]
        peaks = kept.pop(head)
        peak = jnp.maximum(peaks[0], peaks[1])
        weights = [jnp.exp2(p - peak) for p in peaks]
        inverse = 1.0 / (parts[0][64:65] * weights[0] + parts[1][64:65] * weights[1])
        weights = [w * inverse for w in weights]
        r.fac[head, 0:1, :] = weights[0]
        r.fac[head, 1:2, :] = weights[1]
        r.o_t[rows, :] = (parts[0][:64] * weights[0] + parts[1][:64] * weights[1]).astype(BF)
        if head % 2:
            cols = at(head // 2 * 128, 128)
            r.att[:, cols] = r.o_t[cols, :].T

    for head in range(first, first + count):
        scores(head)
        if head > first:
            gather(head - 1)
    gather(first + count - 1)


def big_dot(z, base, left, right, form, finish):
    rows = at(base, CHUNK)
    for n in range(0, z.width, 256):

        def unit(n=n):
            cols = at(n, 256)
            weights = right[:, cols] if form is nn else right[cols, :]
            finish(rows, cols, form(left[rows, :], weights))

        yield unit


def branch_out(z, r, index, base, left, right, before):
    def finish(rows, cols, product):
        value = product + r.branch_bias[index : index + 1, cols].astype(F32)
        r.br_l[index, rows, cols] = value.astype(BF)
        r.tmp[rows, cols] = value + before[rows, cols].astype(F32)

    return big_dot(z, base, left, right, nn, finish)


def adapt(z, r, index, base):
    def inner():
        rows = at(base, CHUNK)
        value, grade = gelu_parts(
            nt(r.br_l[index, rows, :], r.down_l[index]) + r.down_bias[index : index + 1, :]
        )
        low = value.astype(BF)
        r.act[index, rows, 0:64] = low
        r.gd[index, rows, :] = grade
        for n in range(0, z.width, 256):
            cols = at(n, 256)
            r.tmp[rows, cols] += nn(low, r.up_l[index, :, cols]) + r.up_bias[index : index + 1, cols]

    yield inner


def first_norm(z, r, base):
    yield from adapt(z, r, 0, base)
    for row in range(base, base + CHUNK, SUB):

        def unit(row=row):
            rows = at(row, SUB)
            normed, scale = normalize(r.tmp[rows, :])
            r.normed[rows, :] = normed
            r.scale_s[rows, :] = scale
            first = normed * r.norms[0:1, :] + r.norms[1:2, :]
            r.first_f[rows, :] = first
            r.first_l[rows, :] = first.astype(BF)

        yield unit


def expand(z, r, side, base):
    bias = (r.bias_own, r.bias_far)[side]
    rows = at(base, CHUNK)
    for j in range(0, z.ff_half, 256):

        def unit(j=j):
            cols = at(side * z.ff_half + j, 256)
            before = nn(r.first_l[rows, :], r.we[:, cols]) + bias[2:3, at(j, 256)]
            value, grade = gelu_parts(before)
            r.hid[rows, cols] = value.astype(BF)
            r.slope[rows, cols] = grade.astype(BF)

        yield unit


def unshrink(z, r, base):
    rows = at(base, CHUNK)
    for j in range(0, z.ff, 256):

        def unit(j=j):
            cols = at(j, 256)
            grad = nt(r.sgl[rows, :], r.ws[cols, :])
            r.hid[rows, cols] = (grad * r.slope[rows, cols].astype(F32)).astype(BF)

        yield unit


def norm_back(sums, grad, unit, scale, gain):
    for place, part in enumerate((fold_rows(grad * unit), fold_rows(grad))):
        sums[place] = part if sums[place] is None else sums[place] + part
    inner = grad * gain
    back = scale * (
        inner
        - jnp.mean(inner, axis=-1, keepdims=True)
        - unit * jnp.mean(inner * unit, axis=-1, keepdims=True)
    )
    return back, back.astype(BF)


def adapter_out(z, r, index, base, sums):
    def inner():
        rows = at(base, CHUNK)
        low = (nt(r.gl[rows, :], r.up_l[index]) * r.gd[index, rows, :]).astype(BF)
        r.inl[rows, :] = low
        for n in range(0, z.width, 256):
            cols = at(n, 256)
            r.sgl[rows, cols] = (r.ssg[rows, cols] + nn(low, r.down_l[index, :, cols])).astype(BF)
        for place in range(2):
            lines = at((2 * index + place) * 8, 8)
            r.acc[lines, :] = sums[place] if base == 0 else r.acc[lines, :] + sums[place]

    yield inner


def second_norm(z, r, base):
    yield from adapt(z, r, 1, base)
    sums = [None, None]
    for row in range(base, base + CHUNK, SUB):

        def unit(row=row):
            rows = at(row, SUB)
            normed, scale = normalize(r.tmp[rows, :])
            r.output[rows, :] = normed * r.norms[2:3, :] + r.norms[3:4, :]
            back, low = norm_back(
                sums, r.cots[rows, :].astype(F32), normed, scale, r.norms[2:3, :]
            )
            r.ssg[rows, :] = back
            r.gl[rows, :] = low

        yield unit
    yield from adapter_out(z, r, 1, base, sums)


def first_out(z, r, base):
    def finish(rows, cols, product):
        r.tmp[rows, cols] = product + r.ssg[rows, cols]

    return big_dot(z, base, r.hid, r.we, nt, finish)


def first_back(z, r, base):
    sums = [None, None]
    for row in range(base, base + CHUNK, SUB):

        def unit(row=row):
            rows = at(row, SUB)
            back, low = norm_back(
                sums, r.tmp[rows, :], r.normed[rows, :], r.scale_s[rows, :], r.norms[0:1, :]
            )
            r.ssg[rows, :] = back
            r.gl[rows, :] = low

        yield unit
    yield from adapter_out(z, r, 0, base, sums)


def collect(z, r, index):
    def down():
        r.grads[index, 0, 0:64, :] = tn(r.inl[...], r.br_l[index])

    def up():
        r.grads[index, 1, 0:72, :] = tn(r.act[index], r.gl[...])[0:72]

    def lines():
        for place in range(2):
            line = jnp.sum(r.acc[at((2 * index + place) * 8, 8), :], axis=0, keepdims=True)
            r.grads[index, 0, 64 + place : 65 + place, :] = line
        r.grads[index, 1, 65:66, 0:64] = jnp.sum(r.inl[...].astype(F32), axis=0, keepdims=True)

    yield down
    yield up
    yield lines


def branch_back(z, r, base):
    for row in range(0, z.width, 256):

        def unit(row=row):
            rows = at(row, 256)
            r.dat[rows, at(base, CHUNK)] = nt(r.wo[rows, :], r.sgl[at(base, CHUNK), :]).astype(BF)

        yield unit


def attend_back(z, r, pair):
    span = z.tok // 2
    cols = at(pair * 128, 128)
    values = r.values[:, cols]
    got = [[], [], []]
    for j in range(2):
        head = pair * 2 + j
        rows = at(pair * 128 + j * 64, 64)
        grad = r.dat[rows, :].astype(F32)
        dot = jnp.sum(grad * r.o_t[rows, :].astype(F32), axis=0, keepdims=True)
        score_grads = []
        value_grads = []
        for kh in range(2):
            weight = r.fac[head, kh : kh + 1, :]
            scaled = (grad * weight).astype(BF)
            pieces = [scaled, jnp.zeros((64, z.tok), BF)]
            spread = jnp.concatenate(pieces if j == 0 else pieces[::-1], axis=0)
            back = nn(values[kh * span : (kh + 1) * span], spread)
            exps = r.ex[head, at(kh * span, span), :]
            score_grads.append((exps.astype(F32) * (back - dot * weight)).astype(BF))
            value_grads.append(nt(scaled, exps))
        scores = jnp.concatenate(score_grads, axis=0)
        got[0].append((nn(r.k_t[rows, :], scores) * (HEAD_DIM ** -0.5)).astype(BF))
        got[1].append(nt(r.q_t[rows, :], scores).astype(BF))
        got[2].append(jnp.concatenate(value_grads, axis=1).astype(BF))
    pairs_half = z.half // 128
    side = lax.div(pair, pairs_half)
    offset = side * 3 * z.half + lax.rem(pair, pairs_half) * 128
    for c in range(3):
        r.dqkv[:, at(offset + c * z.half, 128)] = jnp.concatenate(got[c], axis=0).T


def input_back(z, r, base):
    rows = at(base, CHUNK)
    r.input_grad[rows, :] = r.ssg[rows, :] + nt(r.dqkv[rows, 0 : 6 * z.half], r.w3[...])


def share(r):
    r.dqkv, r.dat, r.sgl, r.gl, r.ssg = r.slope, r.v_t, r.first_l, r.att, r.first_f


def layer_kernel(z, *refs):
    names = [name for name, _ in INPUTS] + ["output", "input_grad", "sums"]
    names += [f"held{index}" for index in range(15)]
    names += [name for name, _ in SCRATCH] + [name for name, _ in SEMAPHORES]
    r = types.SimpleNamespace(**dict(zip(names, refs, strict=True)))
    share(r)
    tok, width, half, ff_half, n_dp, piece = z.tok, z.width, z.half, z.ff_half, z.n_dp, z.piece
    wide = 3 * half
    dp = lax.axis_index("dp")
    mp = lax.axis_index("mp")
    mate = (dp, 1 - mp)

    def load(src, dst, index):
        copy = pltpu.make_async_copy(src, dst, r.load_sem.at[index])
        copy.start()
        return copy

    load_x = load(r.tokens, r.xs, 0)
    load_w3 = [load(r.triple.at[c], r.w3.at[:, at(c * half, half)], 1 + c) for c in range(3)]

    barrier = pltpu.get_barrier_semaphore()
    ready, go = r.meet.at[0], r.meet.at[1]

    @pl.when(mp == 0)
    def call():
        pl.semaphore_signal(barrier, inc=1, device_id=mate, device_id_type=MESH)

    load_down = load(r.param0, r.held0, 4)
    load_up = load(r.param6, r.held6, 5)
    load_wo = load(r.out_w, r.wo.at[at(0, half), :], 6)
    load_we = load(r.expand, r.we.at[:, at(0, ff_half)], 7)
    load_ws = load(r.shrink, r.ws.at[at(0, ff_half), :], 8)
    load_cot = load(r.cot, r.cots, 9)

    r.bias_own[...] = jnp.zeros_like(r.bias_own)
    r.bias_own[0:2, 0:half] = r.qv_bias[...].astype(F32)
    r.bias_own[2:3, :] = r.expand_bias[...].astype(F32).reshape(1, ff_half)

    ends = []
    total = jnp.int32(0)
    for slot in range(SLOTS - 1):
        total = total + jnp.where(mp == 0, r.lengths[0, slot], r.lengths[1, slot])
        ends.append(total)

    @pl.when(mp == 1)
    def answer():
        pl.semaphore_wait(barrier, 1)
        pl.semaphore_signal(ready, inc=1, device_id=mate, device_id_type=MESH)

    @pl.when(mp == 0)
    def hear():
        pl.semaphore_wait(ready, 1)

        def greet(step, carry):
            peer = lax.rem(dp + step, n_dp)
            pl.semaphore_signal(barrier, inc=1, device_id=(peer, mp), device_id_type=MESH)
            return carry

        lax.fori_loop(1, n_dp, greet, 0)

    def gather_all():
        @pl.when(mp == 0)
        def first_core():
            pl.semaphore_wait(barrier, n_dp - 1)
            pl.semaphore_signal(go, inc=1, device_id=mate, device_id_type=MESH)

        @pl.when(mp == 1)
        def second_core():
            pl.semaphore_wait(go, 1)

    def push(src, dst, index):
        copy = pltpu.make_async_remote_copy(
            src_ref=src,
            dst_ref=dst,
            send_sem=r.far_send.at[index],
            recv_sem=r.far_recv.at[index],
            device_id=mate,
            device_id_type=MESH,
        )
        copy.start()
        return copy

    far_bias = push(r.bias_own, r.bias_far, 0)
    far_w3 = [
        push(r.triple.at[c], r.w3.at[:, at(wide + c * half, half)], 1 + c) for c in range(3)
    ]
    set_masks(z, r, ends)
    r.grads[...] = jnp.zeros_like(r.grads)
    marker = lax.broadcasted_iota(jnp.int32, (tok, 128), 1) == 64
    for index in range(2):
        r.act[index] = jnp.where(marker, 1.0, 0.0).astype(BF)
    load_x.wait()
    for copy in load_w3:
        copy.wait()
    project(z, r, 0)
    far_wo = push(r.out_w, r.wo.at[at(half, half), :], 4)
    far_we = push(r.expand, r.we.at[:, at(ff_half, ff_half)], 5)
    attend(z, r, 0)
    far_ws = push(r.shrink, r.ws.at[at(ff_half, ff_half), :], 6)
    far_bias.wait()
    for copy in far_w3:
        copy.wait()
    project(z, r, 1)
    attend(z, r, 1)

    load_down.wait()
    load_up.wait()
    r.down_l[...] = r.held0[...].astype(BF)
    r.up_l[...] = r.held6[...].astype(BF)
    held = [
        load(getattr(r, f"param{index}"), getattr(r, f"held{index}"), 10 + index)
        for index in range(15)
        if index not in (0, 6)
    ]
    load_wo.wait()
    far_wo.wait()
    load_we.wait()

    def core_copy(b):
        return pltpu.make_async_remote_copy(
            src_ref=r.grads.at[b, 1 - mp],
            dst_ref=r.c_recv.at[b],
            send_sem=r.core_send.at[2 * b],
            recv_sem=r.core_recv.at[2 * b],
            device_id=mate,
            device_id_type=MESH,
        )

    def ring_start(b, stage):
        def body(step, carry):
            peer = lax.rem(dp + step, n_dp)
            if stage == 0:
                src, dst = r.rs_buf.at[b, peer], r.rs_recv.at[b, step - 1]
            else:
                src, dst = r.ag_buf.at[b, dp], r.ag_buf.at[b, dp]
            pltpu.make_async_remote_copy(
                src_ref=src,
                dst_ref=dst,
                send_sem=r.ring_send.at[2 * b + stage],
                recv_sem=r.ring_recv.at[2 * b + stage],
                device_id=(peer, mp),
                device_id_type=MESH,
            ).start()
            return carry

        lax.fori_loop(1, n_dp, body, 0)

    def ring_wait(b, stage):
        block = r.rs_recv.at[b]
        pltpu.make_async_copy(block, block, r.ring_send.at[2 * b + stage]).wait()
        pltpu.make_async_copy(block, block, r.ring_recv.at[2 * b + stage]).wait()

    def last_copy(b):
        return pltpu.make_async_remote_copy(
            src_ref=r.ag_buf.at[b],
            dst_ref=r.ag_far.at[b],
            send_sem=r.core_send.at[2 * b + 1],
            recv_sem=r.core_recv.at[2 * b + 1],
            device_id=mate,
            device_id_type=MESH,
        )

    def reduce_one(b):
        core_copy(b).start()

    def reduce_two(b):
        core_copy(b).wait()
        mine = (r.grads[b, mp] + r.c_recv[b]).astype(BF)
        blocks = jnp.concatenate(
            [mine[:, c * 128 : (c + 1) * 128] for c in range(width // 128)], axis=0
        )
        spare = n_dp * piece - blocks.shape[0]
        if spare:
            blocks = jnp.concatenate([blocks, jnp.zeros((spare, 128), BF)], axis=0)
        r.rs_buf[b] = blocks.reshape(n_dp, piece, 128)
        ring_start(b, 0)

    def reduce_three(b):
        ring_wait(b, 0)

        def add(step, total):
            return total + r.rs_recv[b, step].astype(F32)

        total = lax.fori_loop(0, n_dp - 1, add, r.rs_buf[b, dp].astype(F32))
        r.ag_buf[b, dp] = total.astype(BF)
        ring_start(b, 1)

    def reduce_four(b):
        ring_wait(b, 1)
        last_copy(b).start()

    def reduce_five(b):
        last_copy(b).wait()

    late = CHUNK
    att, hid = r.att, r.hid
    weave(branch_out(z, r, 0, 0, att, r.wo, r.xs))
    weave(branch_out(z, r, 0, late, att, r.wo, r.xs), first_norm(z, r, 0))
    weave(expand(z, r, 0, 0), first_norm(z, r, late))
    weave(expand(z, r, 0, late))
    far_we.wait()
    weave(expand(z, r, 1, 0))
    weave(expand(z, r, 1, late))
    gather_all()
    load_ws.wait()
    load_cot.wait()
    far_ws.wait()
    weave(branch_out(z, r, 1, 0, hid, r.ws, r.first_f))
    weave(branch_out(z, r, 1, late, hid, r.ws, r.first_f), second_norm(z, r, 0))
    weave(unshrink(z, r, 0), second_norm(z, r, late))
    weave(unshrink(z, r, late), collect(z, r, 1))
    reduce_one(1)
    weave(first_out(z, r, 0))
    reduce_two(1)
    weave(first_out(z, r, late), first_back(z, r, 0))
    weave(branch_back(z, r, 0), first_back(z, r, late))
    weave(collect(z, r, 0), branch_back(z, r, late))
    reduce_one(0)

    def back(pair, carry):
        attend_back(z, r, pair)
        return carry

    pairs = width // 128
    lax.fori_loop(0, 1, back, 0)
    reduce_two(0)
    reduce_three(1)
    lax.fori_loop(1, pairs, back, 0)
    reduce_three(0)
    reduce_four(1)
    for base in range(0, tok, CHUNK):
        input_back(z, r, base)
    for copy in held:
        copy.wait()
    reduce_five(1)
    reduce_four(0)
    for b in range(2):
        r.sums[b, mp] = r.ag_buf[b]
    r.sums[1, 1 - mp] = r.ag_far[1]
    reduce_five(0)
    r.sums[0, 1 - mp] = r.ag_far[0]


def update_kernel(blocks, step, output_src, input_grad_src, sums, *refs):
    params, rest = refs[:15], refs[15:]
    output, input_grad, norm_out = rest[:3]
    targets, news, sem = rest[3:18], rest[18:33], rest[33]
    stores = []

    def store(src, dst):
        copy = pltpu.make_async_copy(src, dst, sem.at[len(stores)])
        copy.start()
        stores.append(copy)

    store(output_src, output)
    store(input_grad_src, input_grad)
    squares = jnp.zeros((8, 128), F32)
    for b in range(2):
        for side in range(2):
            part = sums[b, side].astype(F32)
            squares = squares + fold_rows(part * part)
    squares = jnp.sum(jnp.sum(squares, axis=0, keepdims=True), axis=1, keepdims=True)
    grad_norm = jnp.sqrt(squares)
    norm_out[...] = grad_norm
    clip = jnp.minimum(1.0, CLIP_LIMIT / (grad_norm + 1e-06))
    count = jnp.full((1, 1), step[0], jnp.int32).astype(F32)
    fix_one = 1.0 - jnp.exp2(count * jnp.log2(jnp.full((1, 1), 0.9, F32)))
    fix_two = 1.0 - jnp.exp2(count * jnp.log2(jnp.full((1, 1), 0.999, F32)))
    over_one = 1.0 / fix_one
    over_two = 1.0 / fix_two

    def update(index, where, grad):
        weight, first, second = (params[3 * index + n][where] for n in range(3))
        rate, decay = RATES[index]
        clipped = grad * clip
        first_new = 0.9 * first + 0.1 * clipped
        second_new = 0.999 * second + 0.001 * clipped * clipped
        move = first_new * over_one / (jnp.sqrt(second_new * over_two) + 1e-08)
        if decay:
            move = move + decay * weight
        news[3 * index][where] = weight - rate * move
        news[3 * index + 1][where] = first_new
        news[3 * index + 2][where] = second_new

    for b in range(2):
        lines = []
        for side in range(2):
            tops = []
            for c in range(blocks):
                block = sums[b, side, pl.ds(c * PART, PART), :].astype(F32)
                update(
                    2 * side, (b, slice(None), slice(c * 128, (c + 1) * 128)), block[0:64]
                )
                tops.append(block[64:72])
            lines.append(jnp.concatenate(tops, axis=1))
        update(4, (slice(2 * b, 2 * b + 2), slice(None)), lines[0][0:2])
        update(3, (slice(b, b + 1), slice(None)), lines[1][0:1])
        update(1, (slice(b, b + 1), slice(None)), lines[1][1:2, 0:64])
    for index in range(15):
        store(news[index], targets[index])
    for copy in stores:
        copy.wait()


def per_device(
    n_dp,
    tokens,
    lengths,
    cotangent,
    triple_weight,
    query_value_bias,
    output_weight,
    branch_bias,
    expand_weight,
    expand_bias,
    shrink_weight,
    adapter_down,
    down_bias,
    adapter_up,
    up_bias,
    norm_params,
    adapter_down_first,
    adapter_down_second,
    down_bias_first,
    down_bias_second,
    adapter_up_first,
    adapter_up_second,
    up_bias_first,
    up_bias_second,
    norm_params_first,
    norm_params_second,
    step,
):
    tok, width = tokens.shape
    half = triple_weight.shape[2]
    ff_half = expand_weight.shape[1]
    ff = 2 * ff_half
    heads = 2 * half // HEAD_DIM
    blocks = width // 128
    piece = -(-(PART * blocks) // (16 * n_dp)) * 16
    z = types.SimpleNamespace(
        tok=tok,
        width=width,
        half=half,
        ff_half=ff_half,
        ff=ff,
        heads=heads,
        n_dp=n_dp,
        piece=piece,
    )
    flip = lambda v: jnp.swapaxes(v, 1, 2)
    spaces = {
        "s": pl.BlockSpec(memory_space=pltpu.SMEM),
        "v": pl.BlockSpec(memory_space=pltpu.VMEM),
        "h": pl.BlockSpec(memory_space=pltpu.HBM),
    }
    vmem, smem, hbm = spaces["v"], spaces["s"], spaces["h"]
    params = (
        flip(adapter_down),
        flip(adapter_down_first),
        flip(adapter_down_second),
        down_bias,
        down_bias_first,
        down_bias_second,
        adapter_up,
        adapter_up_first,
        adapter_up_second,
        up_bias,
        up_bias_first,
        up_bias_second,
        norm_params,
        norm_params_first,
        norm_params_second,
    )
    operands = (
        lengths,
        query_value_bias,
        branch_bias,
        expand_bias,
        down_bias,
        up_bias,
        norm_params,
        tokens,
        cotangent,
        jnp.transpose(triple_weight, (1, 0, 2)),
        output_weight,
        expand_weight,
        shrink_weight,
        *params,
    )
    output, input_grad, sums, *held = pl.pallas_call(
        functools.partial(layer_kernel, z),
        out_shape=(
            pltpu.VMEM((tok, width), F32),
            pltpu.VMEM((tok, width), F32),
            pltpu.VMEM((2, 2, n_dp, piece, 128), BF),
            *(pltpu.VMEM(p.shape, F32) for p in params),
        ),
        in_specs=[spaces[space] for _, space in INPUTS],
        out_specs=(vmem,) * 18,
        scratch_shapes=[pltpu.VMEM(*make(z)) for _, make in SCRATCH]
        + [
            pltpu.SemaphoreType.DMA((count,)) if count else pltpu.SemaphoreType.REGULAR((2,))
            for _, count in SEMAPHORES
        ],
        compiler_params=pltpu.CompilerParams(
            collective_id=0, has_side_effects=True, vmem_limit_bytes=56 * 2**20
        ),
    )(*operands)
    sums = sums.reshape(2, 2, n_dp * piece, 128)
    results = pl.pallas_call(
        functools.partial(update_kernel, blocks),
        out_shape=(
            jax.ShapeDtypeStruct((tok, width), F32),
            jax.ShapeDtypeStruct((tok, width), F32),
            jax.ShapeDtypeStruct((1, 1), F32),
            *(jax.ShapeDtypeStruct(p.shape, F32) for p in params),
        ),
        in_specs=[smem] + [vmem] * 18,
        out_specs=(hbm, hbm, vmem) + (hbm,) * 15,
        scratch_shapes=[pltpu.VMEM(p.shape, F32) for p in params]
        + [pltpu.SemaphoreType.DMA((17,))],
        compiler_params=pltpu.CompilerParams(vmem_limit_bytes=16 * 2**20),
    )(step, output, input_grad, sums, *held)
    news = list(results[3:])
    for index in range(3):
        news[index] = flip(news[index])
    return (results[0], results[1], results[2].reshape(1), *news)


def solution(mesh):
    split = P(("dp", "mp"), None)
    in_specs = (
        split,
        P("dp", None),
        split,
        P(None, None, "mp"),
        P(None, "mp"),
        P("mp", None),
        P(),
        P(None, "mp"),
        P("mp"),
        P("mp", None),
    ) + (P(),) * 16
    out_specs = (split, split) + (P(),) * 16
    return jax.shard_map(
        functools.partial(per_device, mesh.shape["dp"]),
        mesh=mesh,
        in_specs=in_specs,
        out_specs=out_specs,
        check_vma=False,
    )
```

profile of v0, /device:TPU:0, one launch (start us, length us, event | category | flops | bytes accessed | tf_op | source)
XLA Modules:
  0.0 52.3 jit_solution(16969831984968846469)
XLA Ops:
  1.3 47.6 %shard_map.385 = (f32[512,768]{1,0:T(8,128)S(1)}, f32[512,768]{1,0:T(8,128)S(1)}, bf16[2,2,16,32,128]{4,3,2,1,0:T(8,128)(2,1)S(1)}, f32[2,64,768]{2,1,0:T(8,128)...) custom-call(s32[2,8]{1,0:T(2,128)} %refs_0_.1, ...), custom_call_target="tpu_custom_call" | custom-call | tf_op jit(solution)/shard_map/pallas_call | solution.py:843
  48.9 3.1 %shard_map.386 = (f32[512,768]{1,0:T(8,128)}, f32[512,768]{1,0:T(8,128)}, f32[1,1]{1,0:T(1,128)}, f32[2,64,768]{2,1,0:T(8,128)}, f32[2,64,768]{2,1,0:T(8,128)}, ...) custom-call(s32[1]{0:T(128)S(6)} %copy.44.step, ...), custom_call_target="tpu_custom_call" | custom-call | tf_op jit(solution)/shard_map/pallas_call | solution.py:863
where the time goes:
time: 52.5 us; the launch traced here: 52.3 us
  Pallas kernels  50.7 us (97%)
  between operations  1.5 us (3%)
    pallas_call x1, Pallas kernels, per_device(): pl.pallas_call(functools.partial(layer_kernel, z), out_shape=(pltpu.VMEM(...  47.6 us
    pallas_call x1, Pallas kernels, per_device(): pl.pallas_call(functools.partial(update_kernel, blocks), out_shape=(jax.S...  3.14 us

commit v1 on v0

--- a/solution.py
+++ b/solution.py
@@ -108,9 +108,6 @@
     ("qv_bias", "v"),
     ("branch_bias", "v"),
     ("expand_bias", "v"),
-    ("down_bias", "v"),
-    ("up_bias", "v"),
-    ("norms", "v"),
     ("tokens", "h"),
     ("cot", "h"),
     ("triple", "h"),
@@ -164,22 +161,28 @@
 def project(z, r, side):
     bias = (r.bias_own, r.bias_far)[side]
     base = side * 3 * z.half
-    rows = at(side * z.half, z.half)
-    for c in range(3):
-        mixed = nn(r.xs[...], r.w3[:, at(base + c * z.half, z.half)])
-        if c == 0:
-            mixed = mixed + bias[0:1, 0 : z.half]
-        if c == 2:
-            mixed = mixed + bias[1:2, 0 : z.half]
-        low = mixed.astype(BF)
-        if c == 0:
-            r.q_t[rows, :] = (low.astype(F32) * (HEAD_DIM ** -0.5)).astype(BF).T
-        if c == 1:
-            r.keys[:, rows] = low
-            r.k_t[rows, :] = low.T
-        if c == 2:
-            r.values[:, rows] = low
-            r.v_t[rows, :] = low.T
+    for n in range(0, 3 * z.half, 256):
+
+        def unit(n=n):
+            size = min(256, 3 * z.half - n)
+            mixed = nn(r.xs[...], r.w3[:, at(base + n, size)])
+            for start in range(n, n + size, 128):
+                c, col = start // z.half, start % z.half
+                part = mixed[:, start - n : start - n + 128]
+                if c != 1:
+                    part = part + bias[c // 2 : c // 2 + 1, at(col, 128)]
+                low = part.astype(BF)
+                place = at(side * z.half + col, 128)
+                if c == 0:
+                    r.q_t[place, :] = (low.astype(F32) * (HEAD_DIM ** -0.5)).astype(BF).T
+                if c == 1:
+                    r.keys[:, place] = low
+                    r.k_t[place, :] = low.T
+                if c == 2:
+                    r.values[:, place] = low
+                    r.v_t[place, :] = low.T
+
+        yield unit
 
 
 def attend(z, r, side):
@@ -189,22 +192,18 @@
     ones = jnp.ones((16, z.tok), BF)
     kept = {}
 
-    def scores(head):
+    def score(head, kh, c):
         slot = head % 4
-        r.qa[at(slot * 256 + (head % 2) * 64, 64), :] = r.q_t[at(head * 64, 64), :]
-        keys = jnp.concatenate([r.keys[:, at(head // 2 * 128, 128)], r.hot[...]], axis=1)
-        peaks = []
-        for kh in range(2):
-            tops = []
-            for c in range(2):
-                s = nn(keys[kh * span : (kh + 1) * span], r.qa[at(slot * 256, 256), at(c * span, span)])
-                top = jnp.max(s, axis=0, keepdims=True) * LOG2E
-                r.ex[head, at(kh * span, span), at(c * span, span)] = jnp.exp2(
-                    s * LOG2E - top
-                ).astype(BF)
-                tops.append(top)
-            peaks.append(jnp.concatenate(tops, axis=1))
-        kept[head] = peaks
+        if kh == 0 and c == 0:
+            r.qa[at(slot * 256 + head % 2 * 64, 64), :] = r.q_t[at(head * 64, 64), :]
+        part = at(kh * span, span)
+        keys = jnp.concatenate([r.keys[part, at(head // 2 * 128, 128)], r.hot[part, :]], axis=1)
+        return nn(keys, r.qa[at(slot * 256, 256), at(c * span, span)])
+
+    def exponents(head, kh, c, s):
+        top = jnp.max(s, axis=0, keepdims=True) * LOG2E
+        r.ex[head, at(kh * span, span), at(c * span, span)] = jnp.exp2(s * LOG2E - top).astype(BF)
+        kept[head, kh, c] = top
 
     def gather(head):
         rows = at(head * 64, 64)
@@ -213,7 +212,9 @@
             nn(values[:, kh * span : (kh + 1) * span], r.ex[head, at(kh * span, span), :])
             for kh in range(2)
         ]
-        peaks = kept.pop(head)
+        peaks = [
+            jnp.concatenate([kept.pop((head, kh, c)) for c in range(2)], axis=1) for kh in range(2)
+        ]
         peak = jnp.maximum(peaks[0], peaks[1])
         weights = [jnp.exp2(p - peak) for p in peaks]
         inverse = 1.0 / (parts[0][64:65] * weights[0] + parts[1][64:65] * weights[1])
@@ -225,11 +226,21 @@
             cols = at(head // 2 * 128, 128)
             r.att[:, cols] = r.o_t[cols, :].T
 
-    for head in range(first, first + count):
-        scores(head)
-        if head > first:
-            gather(head - 1)
-    gather(first + count - 1)
+    units = [(head, kh, c) for head in range(first, first + count) for kh in range(2) for c in range(2)]
+    ahead = []
+    yield lambda: ahead.append(score(*units[0]))
+    for index, unit in enumerate(units):
+
+        def step(index=index, unit=unit):
+            s = ahead.pop()
+            if index + 1 < len(units):
+                ahead.append(score(*units[index + 1]))
+            exponents(*unit, s)
+            if unit[1:] == (1, 1) and unit[0] > first:
+                gather(unit[0] - 1)
+
+        yield step
+    yield lambda: gather(first + count - 1)
 
 
 def big_dot(z, base, left, right, form, finish):
@@ -251,6 +262,27 @@
         r.tmp[rows, cols] = value + before[rows, cols].astype(F32)
 
     return big_dot(z, base, left, right, nn, finish)
+
+
+def shrink_own(z, r, base):
+    rows = at(base, CHUNK)
+    for n in range(0, z.width, 256):
+
+        def unit(n=n):
+            own = at(0, z.ff_half)
+            r.tmp[rows, at(n, 256)] = nn(r.hid[rows, own], r.ws[own, at(n, 256)])
+
+        yield unit
+
+
+def shrink_far(z, r, base):
+    def finish(rows, cols, product):
+        value = product + r.tmp[rows, cols] + r.branch_bias[1:2, cols].astype(F32)
+        r.br_l[1, rows, cols] = value.astype(BF)
+        r.tmp[rows, cols] = value + r.first_f[rows, cols]
+
+    far = at(z.ff_half, z.ff_half)
+    return big_dot(z, base, r.hid.at[:, far], r.ws.at[far, :], nn, finish)
 
 
 def adapt(z, r, index, base):
@@ -456,6 +488,7 @@
     names += [name for name, _ in SCRATCH] + [name for name, _ in SEMAPHORES]
     r = types.SimpleNamespace(**dict(zip(names, refs, strict=True)))
     share(r)
+    r.down_bias, r.up_bias, r.norms = r.held3, r.held9, r.held12
     tok, width, half, ff_half, n_dp, piece = z.tok, z.width, z.half, z.ff_half, z.n_dp, z.piece
     wide = 3 * half
     dp = lax.axis_index("dp")
@@ -476,13 +509,6 @@
     @pl.when(mp == 0)
     def call():
         pl.semaphore_signal(barrier, inc=1, device_id=mate, device_id_type=MESH)
-
-    load_down = load(r.param0, r.held0, 4)
-    load_up = load(r.param6, r.held6, 5)
-    load_wo = load(r.out_w, r.wo.at[at(0, half), :], 6)
-    load_we = load(r.expand, r.we.at[:, at(0, ff_half)], 7)
-    load_ws = load(r.shrink, r.ws.at[at(0, ff_half), :], 8)
-    load_cot = load(r.cot, r.cots, 9)
 
     r.bias_own[...] = jnp.zeros_like(r.bias_own)
     r.bias_own[0:2, 0:half] = r.qv_bias[...].astype(F32)
@@ -544,16 +570,26 @@
     load_x.wait()
     for copy in load_w3:
         copy.wait()
-    project(z, r, 0)
+    load_down = load(r.param0, r.held0, 4)
+    load_up = load(r.param6, r.held6, 5)
+    load_small = [
+        load(getattr(r, f"param{index}"), getattr(r, f"held{index}"), 10 + index)
+        for index in (3, 9, 12)
+    ]
+    load_wo = load(r.out_w, r.wo.at[at(0, half), :], 6)
+    load_we = load(r.expand, r.we.at[:, at(0, ff_half)], 7)
+    load_ws = load(r.shrink, r.ws.at[at(0, ff_half), :], 8)
+    load_cot = load(r.cot, r.cots, 9)
+    weave(project(z, r, 0))
     far_wo = push(r.out_w, r.wo.at[at(half, half), :], 4)
     far_we = push(r.expand, r.we.at[:, at(ff_half, ff_half)], 5)
-    attend(z, r, 0)
+    weave(attend(z, r, 0))
     far_ws = push(r.shrink, r.ws.at[at(ff_half, ff_half), :], 6)
     far_bias.wait()
     for copy in far_w3:
         copy.wait()
-    project(z, r, 1)
-    attend(z, r, 1)
+    weave(project(z, r, 1))
+    weave(attend(z, r, 1))
 
     load_down.wait()
     load_up.wait()
@@ -562,8 +598,10 @@
     held = [
         load(getattr(r, f"param{index}"), getattr(r, f"held{index}"), 10 + index)
         for index in range(15)
-        if index not in (0, 6)
+        if index not in (0, 3, 6, 9, 12)
     ]
+    for copy in load_small:
+        copy.wait()
     load_wo.wait()
     far_wo.wait()
     load_we.wait()
@@ -629,11 +667,7 @@
 
     def reduce_three(b):
         ring_wait(b, 0)
-
-        def add(step, total):
-            return total + r.rs_recv[b, step].astype(F32)
-
-        total = lax.fori_loop(0, n_dp - 1, add, r.rs_buf[b, dp].astype(F32))
+        total = jnp.sum(r.rs_recv[b].astype(F32), axis=0) + r.rs_buf[b, dp].astype(F32)
         r.ag_buf[b, dp] = total.astype(BF)
         ring_start(b, 1)
 
@@ -645,43 +679,47 @@
         last_copy(b).wait()
 
     late = CHUNK
-    att, hid = r.att, r.hid
+    att = r.att
     weave(branch_out(z, r, 0, 0, att, r.wo, r.xs))
     weave(branch_out(z, r, 0, late, att, r.wo, r.xs), first_norm(z, r, 0))
     weave(expand(z, r, 0, 0), first_norm(z, r, late))
     weave(expand(z, r, 0, late))
+    load_ws.wait()
+    weave(shrink_own(z, r, 0))
+    weave(shrink_own(z, r, late))
+    gather_all()
+    load_cot.wait()
     far_we.wait()
     weave(expand(z, r, 1, 0))
-    weave(expand(z, r, 1, late))
-    gather_all()
-    load_ws.wait()
-    load_cot.wait()
     far_ws.wait()
-    weave(branch_out(z, r, 1, 0, hid, r.ws, r.first_f))
-    weave(branch_out(z, r, 1, late, hid, r.ws, r.first_f), second_norm(z, r, 0))
+    weave(shrink_far(z, r, 0))
+    weave([*expand(z, r, 1, late), *shrink_far(z, r, late)], second_norm(z, r, 0))
     weave(unshrink(z, r, 0), second_norm(z, r, late))
     weave(unshrink(z, r, late), collect(z, r, 1))
     reduce_one(1)
     weave(first_out(z, r, 0))
+    weave(first_out(z, r, late), first_back(z, r, 0))
     reduce_two(1)
-    weave(first_out(z, r, late), first_back(z, r, 0))
     weave(branch_back(z, r, 0), first_back(z, r, late))
-    weave(collect(z, r, 0), branch_back(z, r, late))
+    weave(collect(z, r, 0))
     reduce_one(0)
+    weave(branch_back(z, r, late))
 
     def back(pair, carry):
         attend_back(z, r, pair)
         return carry
 
     pairs = width // 128
+    middle = pairs // 2
     lax.fori_loop(0, 1, back, 0)
     reduce_two(0)
+    lax.fori_loop(1, middle, back, 0)
     reduce_three(1)
-    lax.fori_loop(1, pairs, back, 0)
+    lax.fori_loop(middle, pairs, back, 0)
     reduce_three(0)
-    reduce_four(1)
     for base in range(0, tok, CHUNK):
         input_back(z, r, base)
+    reduce_four(1)
     for copy in held:
         copy.wait()
     reduce_five(1)
@@ -727,28 +765,32 @@
         clipped = grad * clip
         first_new = 0.9 * first + 0.1 * clipped
         second_new = 0.999 * second + 0.001 * clipped * clipped
-        move = first_new * over_one / (jnp.sqrt(second_new * over_two) + 1e-08)
+        square = second_new * over_two
+        root = square * lax.rsqrt(square) + 1e-08
+        guess = pltpu.reciprocal(root, approx=True)
+        move = first_new * over_one * (guess * (2.0 - root * guess))
         if decay:
             move = move + decay * weight
         news[3 * index][where] = weight - rate * move
         news[3 * index + 1][where] = first_new
         news[3 * index + 2][where] = second_new
 
-    for b in range(2):
-        lines = []
-        for side in range(2):
+    lines = {}
+    for side in range(2):
+        for b in range(2):
             tops = []
             for c in range(blocks):
                 block = sums[b, side, pl.ds(c * PART, PART), :].astype(F32)
-                update(
-                    2 * side, (b, slice(None), slice(c * 128, (c + 1) * 128)), block[0:64]
-                )
+                update(2 * side, (b, slice(None), slice(c * 128, (c + 1) * 128)), block[0:64])
                 tops.append(block[64:72])
-            lines.append(jnp.concatenate(tops, axis=1))
-        update(4, (slice(2 * b, 2 * b + 2), slice(None)), lines[0][0:2])
-        update(3, (slice(b, b + 1), slice(None)), lines[1][0:1])
-        update(1, (slice(b, b + 1), slice(None)), lines[1][1:2, 0:64])
-    for index in range(15):
+            lines[b, side] = jnp.concatenate(tops, axis=1)
+        for n in range(3):
+            store(news[6 * side + n], targets[6 * side + n])
+    for b in range(2):
+        update(4, (slice(2 * b, 2 * b + 2), slice(None)), lines[b, 0][0:2])
+        update(3, (slice(b, b + 1), slice(None)), lines[b, 1][0:1])
+        update(1, (slice(b, b + 1), slice(None)), lines[b, 1][1:2, 0:64])
+    for index in (3, 4, 5, 9, 10, 11, 12, 13, 14):
         store(news[index], targets[index])
     for copy in stores:
         copy.wait()
@@ -829,9 +871,6 @@
         query_value_bias,
         branch_bias,
         expand_bias,
-        down_bias,
-        up_bias,
-        norm_params,
         tokens,
         cotangent,
         jnp.transpose(triple_weight, (1, 0, 2)),

time: 52.5 us -> 50.8 us (0.968)
  Pallas kernels: 50.7 us -> 49.1 us
    pallas_call x1, Pallas kernels: 47.6 us -> 46 us  [per_device(): pl.pallas_call(functools.partial(layer_kernel, z), out_shape=(pltpu.VMEM(...]
where the time goes in v1:
time: 50.8 us; the launch traced here: 50.6 us
  Pallas kernels  49.1 us (97%)
  between operations  1.5 us (3%)
    pallas_call x1, Pallas kernels, per_device(): pl.pallas_call(functools.partial(layer_kernel, z), out_shape=(pltpu.VMEM(...  46 us
    pallas_call x1, Pallas kernels, per_device(): pl.pallas_call(functools.partial(update_kernel, blocks), out_shape=(jax.S...  3.14 us

profile of v1, /device:TPU:0, one launch (start us, length us, event | category | flops | bytes accessed | tf_op | source)
XLA Modules:
  0.0 50.6 jit_solution(18317641484215101946)
XLA Ops:
  1.3 46.0 %shard_map.385 = (f32[512,768]{1,0:T(8,128)S(1)}, f32[512,768]{1,0:T(8,128)S(1)}, bf16[2,2,16,32,128]{4,3,2,1,0:T(8,128)(2,1)S(1)}, f32[2,64,768]{2,1,0:T(8,128)...) custom-call(s32[2,8]{1,0:T(2,128)} %refs_0_.1, ...), custom_call_target="tpu_custom_call" | custom-call | tf_op jit(solution)/shard_map/pallas_call | solution.py:882
  47.3 3.1 %shard_map.386 = (f32[512,768]{1,0:T(8,128)}, f32[512,768]{1,0:T(8,128)}, f32[1,1]{1,0:T(1,128)}, f32[2,64,768]{2,1,0:T(8,128)}, f32[2,64,768]{2,1,0:T(8,128)}, ...) custom-call(s32[1]{0:T(128)S(6)} %copy.44.step, ...), custom_call_target="tpu_custom_call" | custom-call | tf_op jit(solution)/shard_map/pallas_call | solution.py:902

commit v2 on v1

--- a/solution.py
+++ b/solution.py
@@ -53,6 +53,9 @@
 
 
 SCRATCH = (
+    ("qv_bias", lambda z: ((2, z.half), BF)),
+    ("branch_bias", lambda z: ((2, z.width), BF)),
+    ("expand_bias", lambda z: ((z.ff_half,), BF)),
     ("xs", lambda z: ((z.tok, z.width), BF)),
     ("cots", lambda z: ((z.tok, z.width), BF)),
     ("w3", lambda z: ((z.width, 6 * z.half), BF)),
@@ -94,7 +97,7 @@
     ("ag_far", lambda z: ((2, z.n_dp, z.piece, 128), BF)),
 )
 SEMAPHORES = (
-    ("load_sem", 25),
+    ("load_sem", 29),
     ("meet", 0),
     ("far_send", 7),
     ("far_recv", 7),
@@ -104,10 +107,10 @@
     ("ring_recv", 4),
 )
 INPUTS = (
-    ("lengths", "s"),
-    ("qv_bias", "v"),
-    ("branch_bias", "v"),
-    ("expand_bias", "v"),
+    ("lengths_hbm", "h"),
+    ("qv_hbm", "h"),
+    ("branch_hbm", "h"),
+    ("expand_b_hbm", "h"),
     ("tokens", "h"),
     ("cot", "h"),
     ("triple", "h"),
@@ -485,7 +488,7 @@
 def layer_kernel(z, *refs):
     names = [name for name, _ in INPUTS] + ["output", "input_grad", "sums"]
     names += [f"held{index}" for index in range(15)]
-    names += [name for name, _ in SCRATCH] + [name for name, _ in SEMAPHORES]
+    names += [name for name, _ in SCRATCH] + [name for name, _ in SEMAPHORES] + ["lengths"]
     r = types.SimpleNamespace(**dict(zip(names, refs, strict=True)))
     share(r)
     r.down_bias, r.up_bias, r.norms = r.held3, r.held9, r.held12
@@ -503,22 +506,18 @@
     load_x = load(r.tokens, r.xs, 0)
     load_w3 = [load(r.triple.at[c], r.w3.at[:, at(c * half, half)], 1 + c) for c in range(3)]
 
+    load_tiny = [
+        load(r.lengths_hbm, r.lengths, 25),
+        load(r.qv_hbm, r.qv_bias, 26),
+        load(r.expand_b_hbm, r.expand_bias, 27),
+        load(r.branch_hbm, r.branch_bias, 28),
+    ]
     barrier = pltpu.get_barrier_semaphore()
     ready, go = r.meet.at[0], r.meet.at[1]
 
     @pl.when(mp == 0)
     def call():
         pl.semaphore_signal(barrier, inc=1, device_id=mate, device_id_type=MESH)
-
-    r.bias_own[...] = jnp.zeros_like(r.bias_own)
-    r.bias_own[0:2, 0:half] = r.qv_bias[...].astype(F32)
-    r.bias_own[2:3, :] = r.expand_bias[...].astype(F32).reshape(1, ff_half)
-
-    ends = []
-    total = jnp.int32(0)
-    for slot in range(SLOTS - 1):
-        total = total + jnp.where(mp == 0, r.lengths[0, slot], r.lengths[1, slot])
-        ends.append(total)
 
     @pl.when(mp == 1)
     def answer():
@@ -528,23 +527,6 @@
     @pl.when(mp == 0)
     def hear():
         pl.semaphore_wait(ready, 1)
-
-        def greet(step, carry):
-            peer = lax.rem(dp + step, n_dp)
-            pl.semaphore_signal(barrier, inc=1, device_id=(peer, mp), device_id_type=MESH)
-            return carry
-
-        lax.fori_loop(1, n_dp, greet, 0)
-
-    def gather_all():
-        @pl.when(mp == 0)
-        def first_core():
-            pl.semaphore_wait(barrier, n_dp - 1)
-            pl.semaphore_signal(go, inc=1, device_id=mate, device_id_type=MESH)
-
-        @pl.when(mp == 1)
-        def second_core():
-            pl.semaphore_wait(go, 1)
 
     def push(src, dst, index):
         copy = pltpu.make_async_remote_copy(
@@ -558,10 +540,43 @@
         copy.start()
         return copy
 
-    far_bias = push(r.bias_own, r.bias_far, 0)
     far_w3 = [
         push(r.triple.at[c], r.w3.at[:, at(wide + c * half, half)], 1 + c) for c in range(3)
     ]
+
+    @pl.when(mp == 0)
+    def greet_all():
+        def greet(step, carry):
+            peer = lax.rem(dp + step, n_dp)
+            pl.semaphore_signal(barrier, inc=1, device_id=(peer, mp), device_id_type=MESH)
+            return carry
+
+        lax.fori_loop(1, n_dp, greet, 0)
+
+    for copy in load_tiny:
+        copy.wait()
+
+    r.bias_own[...] = jnp.zeros_like(r.bias_own)
+    r.bias_own[0:2, 0:half] = r.qv_bias[...].astype(F32)
+    r.bias_own[2:3, :] = r.expand_bias[...].astype(F32).reshape(1, ff_half)
+
+    ends = []
+    total = jnp.int32(0)
+    for slot in range(SLOTS - 1):
+        total = total + jnp.where(mp == 0, r.lengths[0, slot], r.lengths[1, slot])
+        ends.append(total)
+
+    def gather_all():
+        @pl.when(mp == 0)
+        def first_core():
+            pl.semaphore_wait(barrier, n_dp - 1)
+            pl.semaphore_signal(go, inc=1, device_id=mate, device_id_type=MESH)
+
+        @pl.when(mp == 1)
+        def second_core():
+            pl.semaphore_wait(go, 1)
+
+    far_bias = push(r.bias_own, r.bias_far, 0)
     set_masks(z, r, ends)
     r.grads[...] = jnp.zeros_like(r.grads)
     marker = lax.broadcasted_iota(jnp.int32, (tok, 128), 1) == 64
@@ -715,8 +730,9 @@
     reduce_two(0)
     lax.fori_loop(1, middle, back, 0)
     reduce_three(1)
-    lax.fori_loop(middle, pairs, back, 0)
+    lax.fori_loop(middle, pairs - 1, back, 0)
     reduce_three(0)
+    lax.fori_loop(pairs - 1, pairs, back, 0)
     for base in range(0, tok, CHUNK):
         input_back(z, r, base)
     reduce_four(1)
@@ -765,10 +781,7 @@
         clipped = grad * clip
         first_new = 0.9 * first + 0.1 * clipped
         second_new = 0.999 * second + 0.001 * clipped * clipped
-        square = second_new * over_two
-        root = square * lax.rsqrt(square) + 1e-08
-        guess = pltpu.reciprocal(root, approx=True)
-        move = first_new * over_one * (guess * (2.0 - root * guess))
+        move = first_new * over_one / (jnp.sqrt(second_new * over_two) + 1e-08)
         if decay:
             move = move + decay * weight
         news[3 * index][where] = weight - rate * move
@@ -893,7 +906,8 @@
         + [
             pltpu.SemaphoreType.DMA((count,)) if count else pltpu.SemaphoreType.REGULAR((2,))
             for _, count in SEMAPHORES
-        ],
+        ]
+        + [pltpu.SMEM(lengths.shape, jnp.int32)],
         compiler_params=pltpu.CompilerParams(
             collective_id=0, has_side_effects=True, vmem_limit_bytes=56 * 2**20
         ),

time: 50.8 us -> 48.9 us (0.963)
  Pallas kernels: 49.1 us -> 47.2 us
    pallas_call x1, Pallas kernels: 46 us -> 44.1 us  [per_device(): pl.pallas_call(functools.partial(layer_kernel, z), out_shape=(pltpu.VMEM(...]
where the time goes in v2:
time: 48.9 us; the launch traced here: 48.7 us
  Pallas kernels  47.2 us (97%)
  between operations  1.5 us (3%)
    pallas_call x1, Pallas kernels, per_device(): pl.pallas_call(functools.partial(layer_kernel, z), out_shape=(pltpu.VMEM(...  44.1 us
    pallas_call x1, Pallas kernels, per_device(): pl.pallas_call(functools.partial(update_kernel, blocks), out_shape=(jax.S...  3.14 us

profile of v2, /device:TPU:0, one launch (start us, length us, event | category | flops | bytes accessed | tf_op | source)
XLA Modules:
  0.0 48.7 jit_solution(4193902509932795367)
XLA Ops:
  1.3 44.1 %shard_map.385 = (f32[512,768]{1,0:T(8,128)S(1)}, f32[512,768]{1,0:T(8,128)S(1)}, bf16[2,2,16,32,128]{4,3,2,1,0:T(8,128)(2,1)S(1)}, f32[2,64,768]{2,1,0:T(8,128)...) custom-call(s32[2,8]{1,0:T(2,128)} %refs_0_.1, ...), custom_call_target="tpu_custom_call" | custom-call | tf_op jit(solution)/shard_map/pallas_call | solution.py:895
  45.4 3.1 %shard_map.386 = (f32[512,768]{1,0:T(8,128)}, f32[512,768]{1,0:T(8,128)}, f32[1,1]{1,0:T(1,128)}, f32[2,64,768]{2,1,0:T(8,128)}, f32[2,64,768]{2,1,0:T(8,128)}, ...) custom-call(s32[1]{0:T(128)S(6)} %copy.44.step, ...), custom_call_target="tpu_custom_call" | custom-call | tf_op jit(solution)/shard_map/pallas_call | solution.py:916

commit v3 on v2

--- a/solution.py
+++ b/solution.py
@@ -648,7 +648,11 @@
             ).start()
             return carry
 
-        lax.fori_loop(1, n_dp, body, 0)
+        if n_dp > 16:
+            lax.fori_loop(1, n_dp, body, 0)
+        else:
+            for step in range(1, n_dp):
+                body(step, 0)
 
     def ring_wait(b, stage):
         block = r.rs_recv.at[b]

time: 48.9 us -> 48.8 us (level)
  no operation moved by 1% of the time
where the time goes in v3:
time: 48.8 us; the launch traced here: 48.6 us
  Pallas kernels  47.1 us (97%)
  between operations  1.5 us (3%)
    pallas_call x1, Pallas kernels, per_device(): pl.pallas_call(functools.partial(layer_kernel, z), out_shape=(pltpu.VMEM(...  44 us
    pallas_call x1, Pallas kernels, per_device(): pl.pallas_call(functools.partial(update_kernel, blocks), out_shape=(jax.S...  3.14 us

profile of v3, /device:TPU:0, one launch (start us, length us, event | category | flops | bytes accessed | tf_op | source)
XLA Modules:
  0.0 48.6 jit_solution(15976557741633768971)
XLA Ops:
  1.3 44.0 %shard_map.385 = (f32[512,768]{1,0:T(8,128)S(1)}, f32[512,768]{1,0:T(8,128)S(1)}, bf16[2,2,16,32,128]{4,3,2,1,0:T(8,128)(2,1)S(1)}, f32[2,64,768]{2,1,0:T(8,128)...) custom-call(s32[2,8]{1,0:T(2,128)} %refs_0_.1, ...), custom_call_target="tpu_custom_call" | custom-call | tf_op jit(solution)/shard_map/pallas_call | solution.py:899
  45.3 3.1 %shard_map.386 = (f32[512,768]{1,0:T(8,128)}, f32[512,768]{1,0:T(8,128)}, f32[1,1]{1,0:T(1,128)}, f32[2,64,768]{2,1,0:T(8,128)}, f32[2,64,768]{2,1,0:T(8,128)}, ...) custom-call(s32[1]{0:T(128)S(6)} %copy.44.step, ...), custom_call_target="tpu_custom_call" | custom-call | tf_op jit(solution)/shard_map/pallas_call | solution.py:920
